TPU v7x, 32 devices: a whole 2x2x4 slice. The times are simulated.
32 devices in a mesh: col: 32 (over z, y, x, core).
Axes of the slice: x: 2, y: 2, z: 4, core: 2. Of those that a mesh axis runs over, the one named last changes fastest.
Arguments:
- final_adjoint: float32 [7, 50, 4096], P(None, None, 'col'), may hold values from -6 to 6
- states: float32 [3, 7, 50, 4096], P(None, None, None, 'col'), may hold values from 0.05 to 3
- implicit: float32 [50, 50, 4096], P(None, None, 'col'), may hold values from -0.6 to 1
- wet_levels: int32 [4096], P('col'), may hold values from 12 to 50
- tile_rows: int32 [960], P('col'), may hold values from 0 to 1599, as said below
- tile_cols: int32 [960], P('col'), may hold values from 0 to 1599, as said below
- tiles: bfloat16 [960, 128, 128], P('col'), may hold values from -0.3984375 to 0.3984375
- tile_count: int32 [32], P('col'), may hold values from 5 to 30, as said below
Outputs:
- initial_adjoint: float32 [7, 50, 4096], P(None, None, 'col')
Inputs may be any that keep to these rules, and one draw needn't show every extreme that they name: `tile_rows`: a tile slot of device d names a row block of device d. `tile_cols`: a tile's column block lies on a device at most 2 away from the device of its row block. Slots from tile_count on are not part of the matrix; some device fills all 30 slots.
All inputs are finite; a program needn't handle non-finite values.
Results may differ from a plain program's by a relative error of at most 0.0003.
Values sent between devices are 32-bit elements; how exact they have to be, the bound alone decides.
A program may use at most 64 MiB of HBM per device.

v0:
```python
import jax
import jax.numpy as jnp
from jax import lax
from jax.sharding import PartitionSpec as P

STEPS = 3
REACH = 2


time_step = 0.5


def shifted(value, axis, by):
    peers = lax.axis_size(axis)
    pairs = [(i, i + by) for i in range(peers) if 0 <= i + by < peers]
    return lax.ppermute(value, axis, pairs)


def sources(state, light_factor):
    phosphate, dissolved, oxygen, plankton, grazers, detritus, nitrate = [
        state[i] for i in range(7)
    ]
    growth = (
        1.2 * light_factor * plankton * phosphate / (0.03 + phosphate) * nitrate / (0.5 + nitrate)
    )
    grazing = 1.9 * grazers * plankton * plankton / (0.1 + plankton * plankton)
    mortality = 0.03 * plankton * plankton
    remineral = 0.05 * detritus * oxygen / (1.0 + oxygen)
    dop_decay = 0.17 * dissolved
    grazer_loss = 0.05 * grazers * grazers
    return jnp.stack(
        [
            -growth + remineral + dop_decay + 0.3 * grazing,
            0.1 * growth + 0.1 * mortality - dop_decay,
            1.2 * (growth - remineral - dop_decay),
            growth - grazing - mortality,
            0.7 * grazing - grazer_loss,
            grazer_loss + 0.9 * mortality - remineral,
            1.6 * (remineral + dop_decay - growth),
        ]
    )


def shards(final_adjoint, states, implicit, wet_levels, tile_rows, tile_cols, tiles, tile_count):
    tracers, levels, width = final_adjoint.shape
    blocks_dev = levels * width // 128
    slot_count = tiles.shape[0]
    targets = (2 * REACH + 1) * blocks_dev
    highest = lax.Precision.HIGHEST
    device = lax.axis_index("col")
    level_ids = lax.broadcasted_iota(jnp.int32, (levels, width), 0)
    wet_mask = (level_ids < wet_levels[None, :]).astype(jnp.float32)
    light_factor = jnp.exp(
        -0.2 * lax.broadcasted_iota(jnp.int32, (levels, 1), 0).astype(jnp.float32)
    )
    row_local = tile_rows - device * blocks_dev
    col_slot = (tile_cols // blocks_dev - device + REACH) * blocks_dev + tile_cols % blocks_dev
    active = lax.broadcasted_iota(jnp.int32, (slot_count,), 0) < tile_count[0]
    block_marks = lax.broadcasted_iota(jnp.int32, (blocks_dev,), 0).astype(jnp.float32)
    wide_tiles = tiles.astype(jnp.float32)
    pick_rows = (
        row_local[:, None] == lax.broadcasted_iota(jnp.int32, (slot_count, blocks_dev), 1)
    ).astype(jnp.float32)
    place_cols = (
        (col_slot[:, None] == lax.broadcasted_iota(jnp.int32, (slot_count, targets), 1))
        & active[:, None]
    ).astype(jnp.float32)
    adjoint = final_adjoint
    for section in range(STEPS - 1, -1, -1):
        carried = jnp.einsum("klc,tkc->tlc", implicit, adjoint, precision=highest) * wet_mask
        picked = jnp.einsum("sb,tbi->tsi", pick_rows, carried, precision=highest)
        terms = jnp.einsum("tsi,sij->tsj", picked, wide_tiles, precision=highest)
        partial_value = jnp.einsum("sn,tsj->tnj", place_cols, terms, precision=highest)
        partial_value = partial_value.reshape(tracers, 2 * REACH + 1, blocks_dev, 128)
        own_sum = partial_value[:, 2]
        up_one = (partial_value[:, 3], block_marks)
        up_two = (partial_value[:, 4], block_marks)
        down_one = (partial_value[:, 1], block_marks)
        down_two = (partial_value[:, 0], block_marks)
        got_below = shifted((up_one[0], up_one[1]), "col", 1)
        got_above = shifted((down_one[0], down_one[1]), "col", -1)
        got_far_below = shifted((up_two[0], up_two[1]), "col", 2)
        got_far_above = shifted((down_two[0], down_two[1]), "col", -2)
        from_below = got_below[0]
        from_above = got_above[0]
        far_below = got_far_below[0]
        far_above = got_far_above[0]
        summed = own_sum + from_below + from_above + far_below + far_above
        unused, pull_back = jax.vjp(lambda state: sources(state, light_factor), states[section])
        biology = pull_back(carried)[0]
        adjoint = wet_mask * (carried + summed + time_step * biology)
    return adjoint


def solution(mesh):
    in_specs = (
        P(None, None, "col"),
        P(None, None, None, "col"),
        P(None, None, "col"),
        P("col"),
        P("col"),
        P("col"),
        P("col", None, None),
        P("col"),
    )
    out_specs = P(None, None, "col")
    return jax.shard_map(shards, mesh=mesh, in_specs=in_specs, out_specs=out_specs, check_vma=False)
```

profile of v0, /device:TPU:7, one launch (start us, length us, event | category | flops | bytes accessed | tf_op | source)
XLA Modules:
  0.0 95.9 jit_solution(8156830140347942319)
XLA Ops:
  0.8 0.7 fusion.73
  1.4 0.7 fusion.32
  2.1 1.2 %copy.171 = f32[7,50,128]{1,0,2:T(8,128)S(1)} copy(f32[7,50,128]{2,1,0:T(8,128)} %param.8) | data formatting | bytes 358400 | tf_op args[0]
  3.3 5.5 %copy.172 = f32[50,50,128]{1,0,2:T(8,128)} copy(f32[50,50,128]{2,1,0:T(8,128)} %param.10) | data formatting | bytes 2560000 | tf_op args[2]
  8.7 5.3 %fusion.75 = f32[128,7,50]{2,1,0:T(8,128)S(1)} fusion(f32[7,50,128]{1,0,2:T(8,128)S(1)} %copy.171, f32[50,50,128]{1,0,2:T(8,128)} %copy.172), kind=kOutput, calls=%fused_computation.197 | convolution fusion | flops 26880000 | bytes 1638400 | tf_op jit(solution)/shard_map/klc,tkc->tlc/dot_general | solution.py:70
  14.1 0.2 copy.173
  14.4 0.2 convolution_bitcast_fusion.8
  14.6 0.9 convolution_bitcast_fusion.5
  15.5 0.6 convolution_bitcast_fusion.2
  16.1 0.4 copy.226
  16.6 0.1 slice_bitcast_fusion.13
  16.6 3.7 %collective-permute-start = (f32[7,50,128]{2,0,1:T(8,128)S(1)}, f32[7,50,128]{2,0,1:T(8,128)S(1)}, u32[]{:S(2)}, u32[]{:S(2)}) collective-permute-start(f32[7,50,128]{2,0,1:T(8,128)S(1)} %get-tuple-element.34), channel_id=1, source_target_pairs={{0,1},{1,2},{2,3},{3,4},{4,5},{5,6},{6,7},{7,8},{8,9},{9,10},{10,1... | collective-permute-start | bytes 537608 | tf_op jit(solution)/shard_map/ppermute | solution.py:16
  20.3 2.2 %collective-permute-start.3 = (f32[7,50,128]{2,0,1:T(8,128)S(1)}, f32[7,50,128]{2,0,1:T(8,128)S(1)}, u32[]{:S(2)}, u32[]{:S(2)}) collective-permute-start(f32[7,50,128]{2,0,1:T(8,128)S(1)} %get-tuple-element.35), channel_id=1, source_target_pairs={{2,0},{3,1},{4,2},{5,3},{6,4},{7,5},{8,6},{9,7},{10,8},{11,9},{12,... | collective-permute-start | bytes 537608 | tf_op jit(solution)/shard_map/ppermute | solution.py:16
  22.5 4.9 %collective-permute-start.2 = (f32[7,50,128]{2,0,1:T(8,128)S(1)}, f32[7,50,128]{2,0,1:T(8,128)S(1)}, u32[]{:S(2)}, u32[]{:S(2)}) collective-permute-start(f32[7,50,128]{2,0,1:T(8,128)S(1)} %get-tuple-element.36), channel_id=1, source_target_pairs={{0,2},{1,3},{2,4},{3,5},{4,6},{5,7},{6,8},{7,9},{8,10},{9,11},{10,... | collective-permute-start | bytes 537608 | tf_op jit(solution)/shard_map/ppermute | solution.py:16
  27.4 2.1 %collective-permute-start.1 = (f32[7,50,128]{2,0,1:T(8,128)S(1)}, f32[7,50,128]{2,0,1:T(8,128)S(1)}, u32[]{:S(2)}, u32[]{:S(2)}) collective-permute-start(f32[7,50,128]{2,0,1:T(8,128)S(1)} %get-tuple-element.37), channel_id=1, source_target_pairs={{1,0},{2,1},{3,2},{4,3},{5,4},{6,5},{7,6},{8,7},{9,8},{10,9},{11,1... | collective-permute-start | bytes 537608 | tf_op jit(solution)/shard_map/ppermute | solution.py:16
  29.5 1.7 %fusion.74 = (f32[1,1,50,128]{3,2,1,0:T(8,128)}, f32[1,1,50,128]{3,2,1,0:T(8,128)}, f32[1,1,50,128]{3,2,1,0:T(8,128)S(1)}, f32[1,1,50,128]{3,2,1,0:T(8,128)S(1)}...) fusion(f32[3,7,50,128]{3,2,1,0:T(8,128)} %param.9), kind=kLoop, calls=%fused_computation.196 | loop fusion | flops 19200 | bytes 921600 | tf_op jit(solution)/shard_map/jvp()/slice | solution.py:21
  31.2 0.3 multiply_add_fusion.17
  31.6 0.2 multiply_add_fusion.20
  31.7 0.1 multiply_add_fusion.14
  31.9 0.4 multiply_multiply_fusion.2
  32.3 0.1 multiply_add_fusion.15
  32.4 0.9 collective-permute-done.2
  33.3 3.1 %collective-permute-done.1 = f32[7,50,128]{2,0,1:T(8,128)S(1)} collective-permute-done((f32[7,50,128]{2,0,1:T(8,128)S(1)}, f32[7,50,128]{2,0,1:T(8,128)S(1)}, u32[]{:S(2)}, u32[]{:S(2)}) %collective-permute-start.1) | collective-permute-done | bytes 179232 | tf_op jit(solution)/shard_map/ppermute | solution.py:16
  36.4 0.3 fusion.20
  36.7 0.3 copy.189
  36.9 5.3 %fusion.76 = f32[128,7,50]{2,1,0:T(8,128)S(1)} fusion(f32[7,50,128]{1,0,2:T(8,128)S(1)} %copy.189, f32[50,50,128]{1,0,2:T(8,128)} %copy.172), kind=kOutput, calls=%fused_computation.198 | convolution fusion | flops 26880000 | bytes 1638400 | tf_op jit(solution)/shard_map/klc,tkc->tlc/dot_general | solution.py:70
  42.3 0.2 copy.191
  42.5 0.2 convolution_bitcast_fusion.7
  42.8 0.9 multiply_add_fusion.10
  43.7 0.8 multiply_add_fusion.13
  44.5 0.6 copy-done.4
  45.1 0.7 multiply_add_fusion.7
  45.8 0.9 convolution_bitcast_fusion.4
  46.7 0.6 convolution_bitcast_fusion.1
  47.3 0.4 copy.228
  47.8 0.1 slice_bitcast_fusion.8
  47.8 1.9 %collective-permute-start.4 = (f32[7,50,128]{2,0,1:T(8,128)S(1)}, f32[7,50,128]{2,0,1:T(8,128)S(1)}, u32[]{:S(2)}, u32[]{:S(2)}) collective-permute-start(f32[7,50,128]{2,0,1:T(8,128)S(1)} %get-tuple-element.30), channel_id=1, source_target_pairs={{0,1},{1,2},{2,3},{3,4},{4,5},{5,6},{6,7},{7,8},{8,9},{9,10},{10,1... | collective-permute-start | bytes 537608 | tf_op jit(solution)/shard_map/ppermute | solution.py:16
  49.8 1.9 %collective-permute-start.7 = (f32[7,50,128]{2,0,1:T(8,128)S(1)}, f32[7,50,128]{2,0,1:T(8,128)S(1)}, u32[]{:S(2)}, u32[]{:S(2)}) collective-permute-start(f32[7,50,128]{2,0,1:T(8,128)S(1)} %get-tuple-element.31), channel_id=1, source_target_pairs={{2,0},{3,1},{4,2},{5,3},{6,4},{7,5},{8,6},{9,7},{10,8},{11,9},{12,... | collective-permute-start | bytes 537608 | tf_op jit(solution)/shard_map/ppermute | solution.py:16
  51.7 5.3 %collective-permute-start.6 = (f32[7,50,128]{2,0,1:T(8,128)S(1)}, f32[7,50,128]{2,0,1:T(8,128)S(1)}, u32[]{:S(2)}, u32[]{:S(2)}) collective-permute-start(f32[7,50,128]{2,0,1:T(8,128)S(1)} %get-tuple-element.32), channel_id=1, source_target_pairs={{0,2},{1,3},{2,4},{3,5},{4,6},{5,7},{6,8},{7,9},{8,10},{9,11},{10,... | collective-permute-start | bytes 537608 | tf_op jit(solution)/shard_map/ppermute | solution.py:16
  57.0 3.1 %collective-permute-start.5 = (f32[7,50,128]{2,0,1:T(8,128)S(1)}, f32[7,50,128]{2,0,1:T(8,128)S(1)}, u32[]{:S(2)}, u32[]{:S(2)}) collective-permute-start(f32[7,50,128]{2,0,1:T(8,128)S(1)} %get-tuple-element.33), channel_id=1, source_target_pairs={{1,0},{2,1},{3,2},{4,3},{5,4},{6,5},{7,6},{8,7},{9,8},{10,9},{11,1... | collective-permute-start | bytes 537608 | tf_op jit(solution)/shard_map/ppermute | solution.py:16
  60.1 1.2 %multiply_multiply_fusion.1 = (f32[1,50,128]{2,0,1:T(1,128)S(1)}, f32[1,50,128]{2,0,1:T(1,128)S(1)}, f32[1,50,128]{2,0,1:T(1,128)S(1)}, f32[1,50,128]{2,0,1:T(1,128)S(1)}) fusion(f32[1,1,50,128]{3,2,1,0:T(8,128)} %get-tuple-element.45, f32[7,50,128]{2,0,1:T(8,128)S(1)} %bitcast_multiply_fusion.1, f32[1,1,50,128]{3,2,1,0:T(8,128)S(1)} %get-tuple-element.46, ...), kind=kLoop, calls=%fused_computation.140 | loop fusion | flops 294400 | bytes 435400 | tf_op jit(solution)/shard_map/transpose(jvp())/mul | solution.py:28
  61.3 0.8 multiply_add_fusion.8
  62.1 0.7 collective-permute-done.6
  62.8 3.2 %collective-permute-done.5 = f32[7,50,128]{2,0,1:T(8,128)S(1)} collective-permute-done((f32[7,50,128]{2,0,1:T(8,128)S(1)}, f32[7,50,128]{2,0,1:T(8,128)S(1)}, u32[]{:S(2)}, u32[]{:S(2)}) %collective-permute-start.5) | collective-permute-done | bytes 179232 | tf_op jit(solution)/shard_map/ppermute | solution.py:16
  66.0 1.0 %fusion.13 = f32[7,50,128]{2,0,1:T(8,128)S(1)} fusion(f32[7,50,128]{2,0,1:T(8,128)S(1)} %collective-permute-done.7, f32[7,50,128]{2,0,1:T(8,128)S(1)} %collective-permute-done.6, f32[7,50,128]{2,0,1:T(8,128)S(1)} %collective-permute-done.5, f32[7,50,128]{2,0,1:T(8,128)S(1)} %collective-permute-done.4, f32[7,5,50,128]{3,0,2,1:T(8,128)S(1)} %bitcast.353, ...), kind=kLoop, calls=%fused_computation.32 | loop fusion | flops 672000 | bytes 1459200 | tf_op jit(solution)/shard_map/mul | solution.py:91
  67.0 0.3 copy.207
  67.3 5.3 %fusion.77 = f32[128,7,50]{2,1,0:T(8,128)S(1)} fusion(f32[7,50,128]{1,0,2:T(8,128)S(1)} %copy.207, f32[50,50,128]{1,0,2:T(8,128)} %copy.172), kind=kOutput, calls=%fused_computation.199 | convolution fusion | flops 26880000 | bytes 1638400 | tf_op jit(solution)/shard_map/klc,tkc->tlc/dot_general | solution.py:70
  72.6 0.2 copy.209
  72.9 0.2 convolution_bitcast_fusion.6
  73.1 0.9 convolution_bitcast_fusion.3
  74.0 0.6 convolution_bitcast_fusion
  74.6 0.4 copy.230
  75.1 3.7 %collective-permute-start.8 = (f32[7,50,128]{2,0,1:T(8,128)S(1)}, f32[7,50,128]{2,0,1:T(8,128)S(1)}, u32[]{:S(2)}, u32[]{:S(2)}) collective-permute-start(f32[7,50,128]{2,0,1:T(8,128)S(1)} %get-tuple-element.26), channel_id=1, source_target_pairs={{0,1},{1,2},{2,3},{3,4},{4,5},{5,6},{6,7},{7,8},{8,9},{9,10},{10,1... | collective-permute-start | bytes 537608 | tf_op jit(solution)/shard_map/ppermute | solution.py:16
  78.8 1.9 %collective-permute-start.11 = (f32[7,50,128]{2,0,1:T(8,128)S(1)}, f32[7,50,128]{2,0,1:T(8,128)S(1)}, u32[]{:S(2)}, u32[]{:S(2)}) collective-permute-start(f32[7,50,128]{2,0,1:T(8,128)S(1)} %get-tuple-element.27), channel_id=1, source_target_pairs={{2,0},{3,1},{4,2},{5,3},{6,4},{7,5},{8,6},{9,7},{10,8},{11,9},{12,... | collective-permute-start | bytes 537608 | tf_op jit(solution)/shard_map/ppermute | solution.py:16
  80.8 5.2 %collective-permute-start.10 = (f32[7,50,128]{2,0,1:T(8,128)S(1)}, f32[7,50,128]{2,0,1:T(8,128)S(1)}, u32[]{:S(2)}, u32[]{:S(2)}) collective-permute-start(f32[7,50,128]{2,0,1:T(8,128)S(1)} %get-tuple-element.28), channel_id=1, source_target_pairs={{0,2},{1,3},{2,4},{3,5},{4,6},{5,7},{6,8},{7,9},{8,10},{9,11},{10,... | collective-permute-start | bytes 537608 | tf_op jit(solution)/shard_map/ppermute | solution.py:16
  85.9 1.9 %collective-permute-start.9 = (f32[7,50,128]{2,0,1:T(8,128)S(1)}, f32[7,50,128]{2,0,1:T(8,128)S(1)}, u32[]{:S(2)}, u32[]{:S(2)}) collective-permute-start(f32[7,50,128]{2,0,1:T(8,128)S(1)} %get-tuple-element.29), channel_id=1, source_target_pairs={{1,0},{2,1},{3,2},{4,3},{5,4},{6,5},{7,6},{8,7},{9,8},{10,9},{11,1... | collective-permute-start | bytes 537608 | tf_op jit(solution)/shard_map/ppermute | solution.py:16
  87.9 0.3 multiply_add_fusion.3
  88.2 0.2 multiply_add_fusion.6
  88.4 0.5 multiply_multiply_fusion
  88.9 0.1 multiply_add_fusion.1
  89.0 1.7 %collective-permute-done.10 = f32[7,50,128]{2,0,1:T(8,128)S(1)} collective-permute-done((f32[7,50,128]{2,0,1:T(8,128)S(1)}, f32[7,50,128]{2,0,1:T(8,128)S(1)}, u32[]{:S(2)}, u32[]{:S(2)}) %collective-permute-start.10) | collective-permute-done | bytes 179232 | tf_op jit(solution)/shard_map/ppermute | solution.py:16
  90.7 4.2 %collective-permute-done.9 = f32[7,50,128]{2,0,1:T(8,128)S(1)} collective-permute-done((f32[7,50,128]{2,0,1:T(8,128)S(1)}, f32[7,50,128]{2,0,1:T(8,128)S(1)}, u32[]{:S(2)}, u32[]{:S(2)}) %collective-permute-start.9) | collective-permute-done | bytes 179232 | tf_op jit(solution)/shard_map/ppermute | solution.py:16
  94.9 0.2 fusion.6
  95.2 0.7 copy.225
  (26 shorter events, 0.2 us)
Async XLA Ops:
  0.0 14.6 %copy-start = (bf16[30,128,128]{2,1,0:T(8,128)(2,1)S(1)}, bf16[30,128,128]{2,1,0:T(8,128)(2,1)}, u32[]{:S(2)}) copy-start(bf16[30,128,128]{2,1,0:T(8,128)(2,1)} %param.14) | copy-start | bytes 2949124
  8.7 5.6 %copy-start.6 = (s32[30]{0:T(128)S(1)}, s32[30]{0:T(128)}, u32[]{:S(2)}) copy-start(s32[30]{0:T(128)} %param.12) | copy-start | bytes 364
  16.6 15.7 %collective-permute-start = (f32[7,50,128]{2,0,1:T(8,128)S(1)}, f32[7,50,128]{2,0,1:T(8,128)S(1)}, u32[]{:S(2)}, u32[]{:S(2)}) collective-permute-start(f32[7,50,128]{2,0,1:T(8,128)S(1)} %get-tuple-element.34), channel_id=1, source_target_pairs={{0,1},{1,2},{2,3},{3,4},{4,5},{5,6},{6,7},{7,8},{8,9},{9,10},{10,1... | collective-permute-start | bytes 537608 | tf_op jit(solution)/shard_map/ppermute | solution.py:16
  20.3 12.0 %collective-permute-start.3 = (f32[7,50,128]{2,0,1:T(8,128)S(1)}, f32[7,50,128]{2,0,1:T(8,128)S(1)}, u32[]{:S(2)}, u32[]{:S(2)}) collective-permute-start(f32[7,50,128]{2,0,1:T(8,128)S(1)} %get-tuple-element.35), channel_id=1, source_target_pairs={{2,0},{3,1},{4,2},{5,3},{6,4},{7,5},{8,6},{9,7},{10,8},{11,9},{12,... | collective-permute-start | bytes 537608 | tf_op jit(solution)/shard_map/ppermute | solution.py:16
  22.5 10.8 %collective-permute-start.2 = (f32[7,50,128]{2,0,1:T(8,128)S(1)}, f32[7,50,128]{2,0,1:T(8,128)S(1)}, u32[]{:S(2)}, u32[]{:S(2)}) collective-permute-start(f32[7,50,128]{2,0,1:T(8,128)S(1)} %get-tuple-element.36), channel_id=1, source_target_pairs={{0,2},{1,3},{2,4},{3,5},{4,6},{5,7},{6,8},{7,9},{8,10},{9,11},{10,... | collective-permute-start | bytes 537608 | tf_op jit(solution)/shard_map/ppermute | solution.py:16
  27.4 9.0 %collective-permute-start.1 = (f32[7,50,128]{2,0,1:T(8,128)S(1)}, f32[7,50,128]{2,0,1:T(8,128)S(1)}, u32[]{:S(2)}, u32[]{:S(2)}) collective-permute-start(f32[7,50,128]{2,0,1:T(8,128)S(1)} %get-tuple-element.37), channel_id=1, source_target_pairs={{1,0},{2,1},{3,2},{4,3},{5,4},{6,5},{7,6},{8,7},{9,8},{10,9},{11,1... | collective-permute-start | bytes 537608 | tf_op jit(solution)/shard_map/ppermute | solution.py:16
  31.2 11.6 %copy-start.3 = (f32[1,1,50,128]{3,2,1,0:T(8,128)}, f32[1,1,50,128]{3,2,1,0:T(8,128)S(1)}, u32[]{:S(2)}) copy-start(f32[1,1,50,128]{3,2,1,0:T(8,128)S(1)} %get-tuple-element.44) | copy-start | bytes 76804
  44.5 0.6 copy-start.4
  47.8 14.3 %collective-permute-start.4 = (f32[7,50,128]{2,0,1:T(8,128)S(1)}, f32[7,50,128]{2,0,1:T(8,128)S(1)}, u32[]{:S(2)}, u32[]{:S(2)}) collective-permute-start(f32[7,50,128]{2,0,1:T(8,128)S(1)} %get-tuple-element.30), channel_id=1, source_target_pairs={{0,1},{1,2},{2,3},{3,4},{4,5},{5,6},{6,7},{7,8},{8,9},{9,10},{10,1... | collective-permute-start | bytes 537608 | tf_op jit(solution)/shard_map/ppermute | solution.py:16
  49.8 12.3 %collective-permute-start.7 = (f32[7,50,128]{2,0,1:T(8,128)S(1)}, f32[7,50,128]{2,0,1:T(8,128)S(1)}, u32[]{:S(2)}, u32[]{:S(2)}) collective-permute-start(f32[7,50,128]{2,0,1:T(8,128)S(1)} %get-tuple-element.31), channel_id=1, source_target_pairs={{2,0},{3,1},{4,2},{5,3},{6,4},{7,5},{8,6},{9,7},{10,8},{11,9},{12,... | collective-permute-start | bytes 537608 | tf_op jit(solution)/shard_map/ppermute | solution.py:16
  51.7 11.1 %collective-permute-start.6 = (f32[7,50,128]{2,0,1:T(8,128)S(1)}, f32[7,50,128]{2,0,1:T(8,128)S(1)}, u32[]{:S(2)}, u32[]{:S(2)}) collective-permute-start(f32[7,50,128]{2,0,1:T(8,128)S(1)} %get-tuple-element.32), channel_id=1, source_target_pairs={{0,2},{1,3},{2,4},{3,5},{4,6},{5,7},{6,8},{7,9},{8,10},{9,11},{10,... | collective-permute-start | bytes 537608 | tf_op jit(solution)/shard_map/ppermute | solution.py:16
  57.0 9.0 %collective-permute-start.5 = (f32[7,50,128]{2,0,1:T(8,128)S(1)}, f32[7,50,128]{2,0,1:T(8,128)S(1)}, u32[]{:S(2)}, u32[]{:S(2)}) collective-permute-start(f32[7,50,128]{2,0,1:T(8,128)S(1)} %get-tuple-element.33), channel_id=1, source_target_pairs={{1,0},{2,1},{3,2},{4,3},{5,4},{6,5},{7,6},{8,7},{9,8},{10,9},{11,1... | collective-permute-start | bytes 537608 | tf_op jit(solution)/shard_map/ppermute | solution.py:16
  72.6 15.3 %copy-start.2 = (f32[1,1,50,128]{3,2,1,0:T(8,128)S(1)}, f32[1,1,50,128]{3,2,1,0:T(8,128)}, u32[]{:S(2)}) copy-start(f32[1,1,50,128]{3,2,1,0:T(8,128)} %get-tuple-element.38) | copy-start | bytes 76804
  72.8 15.6 %copy-start.1 = (f32[1,1,50,128]{3,2,1,0:T(8,128)S(1)}, f32[1,1,50,128]{3,2,1,0:T(8,128)}, u32[]{:S(2)}) copy-start(f32[1,1,50,128]{3,2,1,0:T(8,128)} %get-tuple-element.39) | copy-start | bytes 76804
  72.9 16.0 %copy-start.5 = (f32[1,1,50,128]{3,2,1,0:T(8,128)S(1)}, f32[1,1,50,128]{3,2,1,0:T(8,128)}, u32[]{:S(2)}) copy-start(f32[1,1,50,128]{3,2,1,0:T(8,128)} %get-tuple-element.55) | copy-start | bytes 76804
  75.1 13.8 %collective-permute-start.8 = (f32[7,50,128]{2,0,1:T(8,128)S(1)}, f32[7,50,128]{2,0,1:T(8,128)S(1)}, u32[]{:S(2)}, u32[]{:S(2)}) collective-permute-start(f32[7,50,128]{2,0,1:T(8,128)S(1)} %get-tuple-element.26), channel_id=1, source_target_pairs={{0,1},{1,2},{2,3},{3,4},{4,5},{5,6},{6,7},{7,8},{8,9},{9,10},{10,1... | collective-permute-start | bytes 537608 | tf_op jit(solution)/shard_map/ppermute | solution.py:16
  78.8 10.1 %collective-permute-start.11 = (f32[7,50,128]{2,0,1:T(8,128)S(1)}, f32[7,50,128]{2,0,1:T(8,128)S(1)}, u32[]{:S(2)}, u32[]{:S(2)}) collective-permute-start(f32[7,50,128]{2,0,1:T(8,128)S(1)} %get-tuple-element.27), channel_id=1, source_target_pairs={{2,0},{3,1},{4,2},{5,3},{6,4},{7,5},{8,6},{9,7},{10,8},{11,9},{12,... | collective-permute-start | bytes 537608 | tf_op jit(solution)/shard_map/ppermute | solution.py:16
  80.8 9.9 %collective-permute-start.10 = (f32[7,50,128]{2,0,1:T(8,128)S(1)}, f32[7,50,128]{2,0,1:T(8,128)S(1)}, u32[]{:S(2)}, u32[]{:S(2)}) collective-permute-start(f32[7,50,128]{2,0,1:T(8,128)S(1)} %get-tuple-element.28), channel_id=1, source_target_pairs={{0,2},{1,3},{2,4},{3,5},{4,6},{5,7},{6,8},{7,9},{8,10},{9,11},{10,... | collective-permute-start | bytes 537608 | tf_op jit(solution)/shard_map/ppermute | solution.py:16
  85.9 9.0 %collective-permute-start.9 = (f32[7,50,128]{2,0,1:T(8,128)S(1)}, f32[7,50,128]{2,0,1:T(8,128)S(1)}, u32[]{:S(2)}, u32[]{:S(2)}) collective-permute-start(f32[7,50,128]{2,0,1:T(8,128)S(1)} %get-tuple-element.29), channel_id=1, source_target_pairs={{1,0},{2,1},{3,2},{4,3},{5,4},{6,5},{7,6},{8,7},{9,8},{10,9},{11,1... | collective-permute-start | bytes 537608 | tf_op jit(solution)/shard_map/ppermute | solution.py:16
where the time goes:
time: 97.2 us; the launch traced here: 95.9 us
  starting transfers between devices  37.8 us (39%)
  matrix products  21.1 us (22%)
  waiting for transfers between devices  13.8 us (14%)
  other arithmetic  11.3 us (12%)
  local copies, waits for them, and re-layouts  10.7 us (11%)
  between operations  1.16 us (1%)
    ppermute x12, starting transfers between devices, shifted(): return lax.ppermute(value, axis, pairs)  37.8 us
    dot_general x3, matrix products, shards(): jnp.einsum('klc,tkc->tlc', implicit, adjoint, precision=highest) * wet_mask  15.9 us
    ppermute x12, waiting for transfers between devices, shifted(): return lax.ppermute(value, axis, pairs)  13.8 us
    unnamed x16, local copies, waits for them, and re-layouts  7.27 us
    dot_general x3, matrix products, shards(): terms = jnp.einsum('tsi,sij->tsj', picked, wide_tiles, precision=highest)  2.64 us
    mul x3, other arithmetic, sources(): remineral = 0.05 * detritus * oxygen / (1.0 + oxygen)  2.05 us
    add_any x5, other arithmetic, sources(): 1.2 * light_factor * plankton * phosphate / (0.03 + phosphate) * nitrate  1.97 us
  transfers between devices with their start and end apart: 12, of which 6 were waited for; matrix products, arithmetic and copies ran while one was open for 6% of the time, Pallas kernels for 0%

commit v1 on v0

v1 whole, which is shorter than its diff:
```python
import functools

import jax
import jax.numpy as jnp
from jax import lax
from jax.experimental import pallas as pl
from jax.experimental.pallas import tpu as pltpu
from jax.sharding import PartitionSpec as P

STEPS = 3
REACH = 2
OFFSETS = (-2, 2, -1, 1)
TIME_STEP = 0.5


def biology(c, s, light):
    phosphate, _, oxygen, plankton, grazers, detritus, nitrate = s
    inv_p = 1.0 / (0.03 + phosphate)
    inv_n = 1.0 / (0.5 + nitrate)
    inv_o = 1.0 / (1.0 + oxygen)
    square = plankton * plankton
    inv_z = 1.0 / (0.1 + square)
    up = phosphate * inv_p
    un = nitrate * inv_n
    c_growth = -c[0] + 0.1 * c[1] + 1.2 * c[2] + c[3] - 1.6 * c[6]
    c_grazing = 0.3 * c[0] - c[3] + 0.7 * c[4]
    c_mortality = 0.1 * c[1] - c[3] + 0.9 * c[5]
    c_remineral = c[0] - 1.2 * c[2] - c[5] + 1.6 * c[6]
    c_decay = c[0] - c[1] - 1.2 * c[2] + 1.6 * c[6]
    c_loss = c[5] - c[4]
    g = c_growth * (1.2 * light)
    gz = g * plankton
    q = 0.05 * c_remineral
    return (
        gz * un * (0.03 * inv_p * inv_p),
        0.17 * c_decay,
        q * detritus * (inv_o * inv_o),
        g * up * un
        + c_grazing * grazers * plankton * (0.38 * inv_z * inv_z)
        + 0.06 * c_mortality * plankton,
        1.9 * c_grazing * square * inv_z + 0.1 * c_loss * grazers,
        q * oxygen * inv_o,
        gz * up * (0.5 * inv_n * inv_n),
    )


def split(x):
    hi = x.astype(jnp.bfloat16)
    lo = (x - hi.astype(jnp.float32)).astype(jnp.bfloat16)
    return hi, lo


def kernel(
    peers, slots, slots_pad, blocks,
    adj_hbm, states_hbm, imp_hbm, wet_ref, rows_ref, cols_ref, tiles_hbm, count_ref,
    out_ref,
    adj, states, imp, tiles, carried, by_block, sent, got, ids, got_ids,
    load_sem, id_send, id_recv, send_sem, recv_sem,
):
    tracers, levels, width = adj.shape
    body = tracers * slots_pad
    by_row = by_block.reshape(blocks * 8, 128)
    me = lax.axis_index("col")

    loads = [
        pltpu.make_async_copy(src, dst, load_sem.at[i])
        for i, (src, dst) in enumerate(
            ((adj_hbm, adj), (imp_hbm, imp), (tiles_hbm, tiles), (states_hbm, states))
        )
    ]
    for load in loads:
        load.start()

    inside = [(me + off >= 0) & (me + off < peers) for off in OFFSETS]

    barrier = pltpu.get_barrier_semaphore()
    for off, ok in zip(OFFSETS, inside):
        @pl.when(ok)
        def _():
            pl.semaphore_signal(
                barrier, inc=1, device_id=(me + off,), device_id_type=pl.DeviceIdType.MESH
            )

    lane_slot = lax.broadcasted_iota(jnp.int32, (8, 128), 1) % slots_pad
    own_ids = jnp.full((8, 128), -1, jnp.int32)
    for s in range(slots):
        own_ids = jnp.where(lane_slot == s, cols_ref[s], own_ids)
    own_ids = jnp.where(lane_slot < count_ref[0], own_ids, -1)
    ids[...] = own_ids
    zero_row = jnp.zeros((8, 128), jnp.float32)
    for n in range(STEPS):
        for s in range(slots, slots_pad):
            sent[n, pl.ds(s, 8, stride=slots_pad), :] = zero_row
    for first in range(0, levels, 8):
        rows = min(8, levels - first)
        by_row[pl.ds(first * 8 + 7, rows, stride=8), :] = jnp.zeros((rows, 128), jnp.float32)

    for i, ok in enumerate(inside):
        @pl.when(jnp.logical_not(ok))
        def _():
            got_ids[i] = jnp.full((8, 128), -1, jnp.int32)
            for n in range(STEPS):
                got[n, i] = jnp.zeros((body, 128), jnp.float32)

    pl.semaphore_wait(barrier, sum(ok.astype(jnp.int32) for ok in inside))

    def place_of(off):
        return OFFSETS.index(-off)

    id_copies = [
        pltpu.make_async_remote_copy(
            src_ref=ids, dst_ref=got_ids.at[place_of(off)],
            send_sem=id_send.at[i], recv_sem=id_recv.at[place_of(off)],
            device_id=(me + off,), device_id_type=pl.DeviceIdType.MESH,
        )
        for i, off in enumerate(OFFSETS)
    ]
    for copy, ok in zip(id_copies, inside):
        pl.when(ok)(copy.start)

    level = lax.broadcasted_iota(jnp.int32, (levels, width), 0)

    def wet(first, rows):
        ids_ = lax.broadcasted_iota(jnp.int32, (rows, width), 0) + first
        return (ids_ < wet_ref[...]).astype(jnp.float32)

    loads[0].wait()
    loads[1].wait()

    block_row = lax.broadcasted_iota(jnp.int32, (blocks, 2 * slots_pad), 0)
    own_pick = (block_row == own_ids[0:1, : 2 * slots_pad] - me * blocks).astype(jnp.bfloat16)
    near_pick = None

    for n in range(STEPS):
        section = STEPS - 1 - n
        for first in range(0, levels, 32):
            rows = min(32, levels - first)
            acc = [None] * tracers
            for k in range(levels):
                m = imp[k, pl.ds(first, rows), :]
                for t in range(tracers):
                    term = m * adj[t, pl.ds(k, 1), :]
                    acc[t] = term if acc[t] is None else acc[t] + term
            mask = wet(first, rows)
            for t in range(tracers):
                value = acc[t] * mask
                carried[t, pl.ds(first, rows), :] = value
                for r in range(0, rows, 8):
                    some = min(8, rows - r)
                    by_row[pl.ds((first + r) * 8 + t, some, stride=8), :] = value[r : r + some]
        if n == 0:
            loads[2].wait()
        for s in range(slots):
            row = jnp.minimum(jnp.maximum(rows_ref[s] - me * blocks, 0), blocks - 1)
            hi, lo = split(by_block[row])
            term = jnp.dot(
                jnp.concatenate([hi, lo], axis=0), tiles[s], preferred_element_type=jnp.float32
            )
            sent[n, pl.ds(s, 8, stride=slots_pad), :] = term[:8] + term[8:]
        copies = [
            pltpu.make_async_remote_copy(
                src_ref=sent.at[n, pl.ds(0, body)], dst_ref=got.at[n, place_of(off)],
                send_sem=send_sem.at[n, i], recv_sem=recv_sem.at[n, place_of(off)],
                device_id=(me + off,), device_id_type=pl.DeviceIdType.MESH,
            )
            for i, off in enumerate(OFFSETS)
        ]
        for copy, ok in zip(copies, inside):
            pl.when(ok)(copy.start)

        if n == 0:
            loads[3].wait()
        own = []
        for t in range(tracers):
            hi, lo = split(sent[n, pl.ds(t * slots_pad, slots_pad), :])
            own.append(jnp.concatenate([hi, lo], axis=0))
        own_sum = jnp.dot(
            own_pick, jnp.concatenate(own, axis=1), preferred_element_type=jnp.float32
        )
        for first in range(0, levels, 8):
            rows = min(8, levels - first)
            part = pl.ds(first, rows)
            mask = wet(first, rows)
            depth = (lax.broadcasted_iota(jnp.int32, (rows, width), 0) + first).astype(jnp.float32)
            light = jnp.exp(-0.2 * depth)
            c = [carried[t, part, :] for t in range(tracers)]
            state = [states[section, t, part, :] for t in range(tracers)]
            bio = biology(c, state, light)
            for t in range(tracers):
                own_part = own_sum[first : first + rows, t * 128 : (t + 1) * 128]
                adj[t, part, :] = mask * (c[t] + own_part + TIME_STEP * bio[t])

        if n == 0:
            for i, off in enumerate(OFFSETS):
                pl.when(inside[i])(id_copies[place_of(off)].wait_recv)
            lanes = lax.broadcasted_iota(jnp.int32, (8, 128), 1) // slots_pad
            near = got_ids[0]
            for i in range(1, len(OFFSETS)):
                near = jnp.where(lanes == i, got_ids[i], near)
            rows_near = lax.broadcasted_iota(jnp.int32, (blocks, 128), 0)
            near_pick = (rows_near == near[0:1] - me * blocks).astype(jnp.bfloat16)
            near_pick = jnp.concatenate([near_pick, near_pick], axis=1)
        for i in range(len(OFFSETS)):
            pl.when(inside[i])(copies[place_of(OFFSETS[i])].wait_recv)
        near_terms = []
        for t in range(tracers):
            pieces = [got[n, i, pl.ds(t * slots_pad, slots_pad), :] for i in range(len(OFFSETS))]
            hi, lo = split(jnp.concatenate(pieces, axis=0))
            near_terms.append(jnp.concatenate([hi, lo], axis=0))
        near_sum = jnp.dot(
            near_pick, jnp.concatenate(near_terms, axis=1), preferred_element_type=jnp.float32
        )
        mask = wet(0, levels)
        for t in range(tracers):
            value = adj[t] + mask * near_sum[:, t * 128 : (t + 1) * 128]
            if n == STEPS - 1:
                out_ref[t] = value
            else:
                adj[t] = value
        for copy, ok in zip(copies, inside):
            pl.when(ok)(copy.wait_send)
    for copy, ok in zip(id_copies, inside):
        pl.when(ok)(copy.wait_send)


def shards(peers, final_adjoint, states, implicit, wet_levels, tile_rows, tile_cols, tiles, tile_count):
    tracers, levels, width = final_adjoint.shape
    blocks = levels * width // 128
    slots = tiles.shape[0]
    slots_pad = -(-slots // 32) * 32
    body = tracers * slots_pad
    near = len(OFFSETS)
    hbm = pl.BlockSpec(memory_space=pl.ANY)
    smem = pl.BlockSpec(memory_space=pltpu.SMEM)
    vmem = pl.BlockSpec(memory_space=pltpu.VMEM)
    f32 = jnp.float32
    return pl.pallas_call(
        functools.partial(kernel, peers, slots, slots_pad, blocks),
        out_shape=jax.ShapeDtypeStruct((tracers, levels, width), f32),
        in_specs=[hbm, hbm, hbm, vmem, smem, smem, hbm, smem],
        out_specs=vmem,
        scratch_shapes=[
            pltpu.VMEM((tracers, levels, width), f32),
            pltpu.VMEM(states.shape, f32),
            pltpu.VMEM(implicit.shape, f32),
            pltpu.VMEM(tiles.shape, tiles.dtype),
            pltpu.VMEM((tracers, levels, width), f32),
            pltpu.VMEM((blocks, 8, 128), f32),
            pltpu.VMEM((STEPS, 8 * slots_pad, 128), f32),
            pltpu.VMEM((STEPS, near, body, 128), f32),
            pltpu.VMEM((8, 128), jnp.int32),
            pltpu.VMEM((near, 8, 128), jnp.int32),
            pltpu.SemaphoreType.DMA((4,)),
            pltpu.SemaphoreType.DMA((near,)),
            pltpu.SemaphoreType.DMA((near,)),
            pltpu.SemaphoreType.DMA((STEPS, near)),
            pltpu.SemaphoreType.DMA((STEPS, near)),
        ],
        compiler_params=pltpu.CompilerParams(
            collective_id=0, has_side_effects=True, vmem_limit_bytes=32 * 1024 * 1024
        ),
    )(
        final_adjoint, states, implicit, wet_levels.reshape(1, width),
        tile_rows, tile_cols, tiles, tile_count,
    )


def solution(mesh):
    in_specs = (
        P(None, None, "col"),
        P(None, None, None, "col"),
        P(None, None, "col"),
        P("col"),
        P("col"),
        P("col"),
        P("col", None, None),
        P("col"),
    )
    out_specs = P(None, None, "col")
    return jax.shard_map(
        functools.partial(shards, mesh.shape["col"]),
        mesh=mesh, in_specs=in_specs, out_specs=out_specs, check_vma=False,
    )
```

time: 97.2 us -> 42.7 us (0.44)
  the two profiles are of different devices: /device:TPU:7 before, /device:TPU:1 now
where the time goes in v1:
time: 42.7 us; the launch traced here: 42.4 us
  Pallas kernels  34.5 us (81%)
  local copies, waits for them, and re-layouts  7.19 us (17%)
  between operations  0.67 us (2%)
    pallas_call x1, Pallas kernels, shards(): pl.pallas_call(functools.partial(kernel, peers, slots, slots_pad, blocks)...  34.5 us
    unnamed x15, local copies, waits for them, and re-layouts  7.19 us

profile of v1, /device:TPU:1, one launch (start us, length us, event | category | flops | bytes accessed | tf_op | source)
XLA Modules:
  0.0 42.4 jit_solution(10570066616909838368)
XLA Ops:
  0.7 0.0 copy-start
  0.7 1.4 %copy-done = f32[50,50,128]{2,1,0:T(8,128)S(1)} copy-done((f32[50,50,128]{2,1,0:T(8,128)S(1)}, f32[50,50,128]{2,1,0:T(8,128)}, u32[]{:S(2)}) %copy-start) | copy-done | bytes 1280024
  2.0 0.0 copy-start.1
  2.0 1.2 %copy-done.1 = bf16[30,128,128]{2,1,0:T(8,128)(2,1)S(1)} copy-done((bf16[30,128,128]{2,1,0:T(8,128)(2,1)S(1)}, bf16[30,128,128]{2,1,0:T(8,128)(2,1)}, u32[]{:S(2)}) %copy-start.1) | copy-done | bytes 983064
  3.2 0.0 copy-start.2
  3.2 1.1 %copy-done.2 = f32[3,7,50,128]{3,2,1,0:T(8,128)S(1)} copy-done((f32[3,7,50,128]{3,2,1,0:T(8,128)S(1)}, f32[3,7,50,128]{3,2,1,0:T(8,128)}, u32[]{:S(2)}) %copy-start.2) | copy-done | bytes 537624
  4.3 0.0 copy-start.3
  4.3 0.9 %copy-done.3 = f32[7,50,128]{2,1,0:T(8,128)S(1)} copy-done((f32[7,50,128]{2,1,0:T(8,128)S(1)}, f32[7,50,128]{2,1,0:T(8,128)}, u32[]{:S(2)}) %copy-start.3) | copy-done | bytes 179224
  5.2 0.0 copy-start.4
  5.2 0.7 %copy-done.4 = s32[128]{0:T(128)S(1)} copy-done((s32[128]{0:T(128)S(1)}, s32[128]{0:T(128)}, u32[]{:S(2)}) %copy-start.4) | copy-done | bytes 536
  5.9 0.0 copy-start.5
  5.9 0.7 %copy-done.5 = s32[30]{0:T(128)S(1)} copy-done((s32[30]{0:T(128)S(1)}, s32[30]{0:T(128)}, u32[]{:S(2)}) %copy-start.5) | copy-done | bytes 144
  6.5 0.0 copy-start.6
  6.5 0.7 %copy-done.6 = s32[30]{0:T(128)S(1)} copy-done((s32[30]{0:T(128)S(1)}, s32[30]{0:T(128)}, u32[]{:S(2)}) %copy-start.6) | copy-done | bytes 144
  7.2 34.5 %shard_map.82 = f32[7,50,128]{2,1,0:T(8,128)S(1)} custom-call(f32[7,50,128]{2,1,0:T(8,128)S(1)} %copy-done.3, f32[3,7,50,128]{3,2,1,0:T(8,128)S(1)} %copy-done.2, f32[50,50,128]{2,1,0:T(8,128)S(1)} %copy-done, s32[1,128]{1,0:T(1,128)S(1)} %bitcast.1, s32[30]{0:T(128)S(1)} %copy-done.5, s32[30]{0:T(128)S(1)} %copy-done.6, ...), custom_call_target="tpu_custom_call" | custom-call | tf_op jit(solution)/shard_map/pallas_call | solution.py:237
  41.7 0.7 %copy.11 = f32[7,50,128]{2,1,0:T(8,128)} copy(f32[7,50,128]{2,1,0:T(8,128)S(1)} %shard_map.82) | data formatting | bytes 358400
Async XLA Ops:
  0.7 1.4 %copy-start = (f32[50,50,128]{2,1,0:T(8,128)S(1)}, f32[50,50,128]{2,1,0:T(8,128)}, u32[]{:S(2)}) copy-start(f32[50,50,128]{2,1,0:T(8,128)} %imp_hbm.1) | copy-start | bytes 3840004
  2.0 1.2 %copy-start.1 = (bf16[30,128,128]{2,1,0:T(8,128)(2,1)S(1)}, bf16[30,128,128]{2,1,0:T(8,128)(2,1)}, u32[]{:S(2)}) copy-start(bf16[30,128,128]{2,1,0:T(8,128)(2,1)} %tiles_hbm.1) | copy-start | bytes 2949124
  3.2 1.1 %copy-start.2 = (f32[3,7,50,128]{3,2,1,0:T(8,128)S(1)}, f32[3,7,50,128]{3,2,1,0:T(8,128)}, u32[]{:S(2)}) copy-start(f32[3,7,50,128]{3,2,1,0:T(8,128)} %states_hbm.1) | copy-start | bytes 1612804
  4.3 0.9 %copy-start.3 = (f32[7,50,128]{2,1,0:T(8,128)S(1)}, f32[7,50,128]{2,1,0:T(8,128)}, u32[]{:S(2)}) copy-start(f32[7,50,128]{2,1,0:T(8,128)} %adj_hbm.1) | copy-start | bytes 537604
  5.2 0.7 %copy-start.4 = (s32[128]{0:T(128)S(1)}, s32[128]{0:T(128)}, u32[]{:S(2)}) copy-start(s32[128]{0:T(128)} %param.11) | copy-start | bytes 1540
  5.9 0.7 %copy-start.5 = (s32[30]{0:T(128)S(1)}, s32[30]{0:T(128)}, u32[]{:S(2)}) copy-start(s32[30]{0:T(128)} %rows_ref.1) | copy-start | bytes 364
  6.5 0.7 %copy-start.6 = (s32[30]{0:T(128)S(1)}, s32[30]{0:T(128)}, u32[]{:S(2)}) copy-start(s32[30]{0:T(128)} %cols_ref.1) | copy-start | bytes 364

commit v2 on v1

v2 whole, which is shorter than its diff:
```python
import functools

import jax
import jax.numpy as jnp
from jax import lax
from jax.experimental import pallas as pl
from jax.experimental.pallas import tpu as pltpu
from jax.sharding import PartitionSpec as P

STEPS = 3
REACH = 2
CHUNK = 8
PARTNER, ACROSS, RELAYED, PASSED = range(4)
TIME_STEP = 0.5


def biology(c, s, light):
    phosphate, _, oxygen, plankton, grazers, detritus, nitrate = s
    inv_p = 1.0 / (0.03 + phosphate)
    inv_n = 1.0 / (0.5 + nitrate)
    inv_o = 1.0 / (1.0 + oxygen)
    square = plankton * plankton
    inv_z = 1.0 / (0.1 + square)
    up = phosphate * inv_p
    un = nitrate * inv_n
    c_growth = -c[0] + 0.1 * c[1] + 1.2 * c[2] + c[3] - 1.6 * c[6]
    c_grazing = 0.3 * c[0] - c[3] + 0.7 * c[4]
    c_mortality = 0.1 * c[1] - c[3] + 0.9 * c[5]
    c_remineral = c[0] - 1.2 * c[2] - c[5] + 1.6 * c[6]
    c_decay = c[0] - c[1] - 1.2 * c[2] + 1.6 * c[6]
    c_loss = c[5] - c[4]
    g = c_growth * (1.2 * light)
    gz = g * plankton
    q = 0.05 * c_remineral
    return (
        gz * un * (0.03 * inv_p * inv_p),
        0.17 * c_decay,
        q * detritus * (inv_o * inv_o),
        g * up * un
        + c_grazing * grazers * plankton * (0.38 * inv_z * inv_z)
        + 0.06 * c_mortality * plankton,
        1.9 * c_grazing * square * inv_z + 0.1 * c_loss * grazers,
        q * oxygen * inv_o,
        gz * up * (0.5 * inv_n * inv_n),
    )


def split(x):
    hi = x.astype(jnp.bfloat16)
    lo = (x - hi.astype(jnp.float32)).astype(jnp.bfloat16)
    return hi, lo


def kernel(
    peers, slots, chunks, blocks,
    adj_hbm, states_hbm, imp_hbm, wet_ref, rows_ref, cols_ref, tiles_hbm, count_ref,
    out_ref,
    adj, states, imp, tiles, carried, by_block, sent, got,
    load_sem, send_sem, recv_sem,
):
    tracers, levels, width = adj.shape
    slots_pad = chunks * CHUNK
    body = tracers * CHUNK
    by_row = by_block.reshape(blocks * 8, 128)
    me = lax.axis_index("col")
    chip = me // 2
    core = me % 2
    odd = chip % 2
    partner = me + 1 - 2 * core
    across = me + 2 - 4 * odd
    relay_to = me + 4 - 8 * odd
    relay_from = me - 4 + 8 * odd
    relays = (relay_to >= 0) & (relay_to < peers)
    relayed = (relay_from >= 0) & (relay_from < peers)
    passes_across = core == odd
    passes_relayed = (core != odd) & relayed
    gets_passed = (core != odd) | relayed
    misses_passed = (core == odd) & jnp.logical_not(relayed)

    loads = [
        pltpu.make_async_copy(src, dst, load_sem.at[i])
        for i, (src, dst) in enumerate(
            ((adj_hbm, adj), (imp_hbm, imp), (tiles_hbm, tiles), (states_hbm, states))
        )
    ]
    for load in loads:
        load.start()

    barrier = pltpu.get_barrier_semaphore()

    def greet(device):
        pl.semaphore_signal(
            barrier, inc=1, device_id=(device,), device_id_type=pl.DeviceIdType.MESH
        )

    greet(partner)
    greet(across)
    pl.when(relays)(lambda: greet(relay_to))
    pl.when(relayed)(lambda: greet(relay_from))

    lane = lax.broadcasted_iota(jnp.int32, (8, 128), 1)
    lane_slot = lane % slots_pad
    own_ids = jnp.full((8, 128), -1, jnp.int32)
    for s in range(slots):
        own_ids = jnp.where(lane_slot == s, cols_ref[s], own_ids)
    own_ids = jnp.where(lane_slot < count_ref[0], own_ids, -1).astype(jnp.float32)
    zero_tile = jnp.zeros((8, 128), jnp.float32)
    for n in range(STEPS):
        for s in range(slots, slots_pad):
            sent[n, s // CHUNK, pl.ds(s % CHUNK, 8, stride=CHUNK), :] = zero_tile
    for first in range(0, levels, 8):
        rows = min(8, levels - first)
        by_row[pl.ds(first * 8 + 7, rows, stride=8), :] = jnp.zeros((rows, 128), jnp.float32)

    def blank(place):
        for n in range(STEPS):
            for q in range(chunks):
                got[n, place, q] = jnp.zeros(got.shape[3:], jnp.float32)
        got[0, place, 0, pl.ds(body, 8), :] = jnp.full((8, 128), -1.0, jnp.float32)

    pl.when(jnp.logical_not(relayed))(lambda: blank(RELAYED))
    pl.when(misses_passed)(lambda: blank(PASSED))

    pl.semaphore_wait(
        barrier, 2 + relays.astype(jnp.int32) + relayed.astype(jnp.int32)
    )

    def copy_of(n, q, source, place, device):
        size = body + (8 if n == 0 and q == 0 else 0)
        return pltpu.make_async_remote_copy(
            src_ref=source.at[pl.ds(0, size)], dst_ref=got.at[n, place, q, pl.ds(0, size)],
            send_sem=send_sem.at[n, place, q], recv_sem=recv_sem.at[n, place, q],
            device_id=(device,), device_id_type=pl.DeviceIdType.MESH,
        )

    def wet(first, rows):
        level = lax.broadcasted_iota(jnp.int32, (rows, width), 0) + first
        return (level < wet_ref[...]).astype(jnp.float32)

    def pick_of(targets):
        block = lax.broadcasted_iota(jnp.int32, (blocks, targets.shape[1]), 0) + me * blocks
        pick = (block.astype(jnp.float32) == targets).astype(jnp.bfloat16)
        return jnp.concatenate([pick, pick], axis=1)

    def placed(pick, sources):
        columns = []
        for t in range(tracers):
            pieces = [ref[q, pl.ds(t * CHUNK, CHUNK), :] for ref in sources for q in range(chunks)]
            columns.append(jnp.concatenate(split(jnp.concatenate(pieces, axis=0)), axis=0))
        return jnp.dot(pick, jnp.concatenate(columns, axis=1), preferred_element_type=jnp.float32)

    loads[0].wait()
    loads[1].wait()
    own_pick = pick_of(own_ids[0:1, :slots_pad])
    near_pick = far_pick = None
    level_parts = [(first, min(8, levels - first)) for first in range(0, levels, 8)]
    per_chunk = -(-len(level_parts) // chunks)
    started = []

    for n in range(STEPS):
        section = STEPS - 1 - n
        for first in range(0, levels, 32):
            rows = min(32, levels - first)
            acc = [None] * tracers
            for k in range(levels):
                m = imp[k, pl.ds(first, rows), :]
                for t in range(tracers):
                    term = m * adj[t, pl.ds(k, 1), :]
                    acc[t] = term if acc[t] is None else acc[t] + term
            mask = wet(first, rows)
            for t in range(tracers):
                value = acc[t] * mask
                carried[t, pl.ds(first, rows), :] = value
                for r in range(0, rows, 8):
                    some = min(8, rows - r)
                    by_row[pl.ds((first + r) * 8 + t, some, stride=8), :] = value[r : r + some]
        if n == 0:
            loads[2].wait()
        for q in range(chunks):
            for s in range(q * CHUNK, min(slots, (q + 1) * CHUNK)):
                row = jnp.minimum(jnp.maximum(rows_ref[s] - me * blocks, 0), blocks - 1)
                hi, lo = split(by_block[row])
                term = jnp.dot(
                    jnp.concatenate([hi, lo], axis=0), tiles[s], preferred_element_type=jnp.float32
                )
                sent[n, q, pl.ds(s % CHUNK, 8, stride=CHUNK), :] = term[:8] + term[8:]
            if n == 0 and q == 0:
                sent[0, 0, pl.ds(body, 8), :] = own_ids
            to_across = copy_of(n, q, sent.at[n, q], ACROSS, across)
            to_partner = copy_of(n, q, sent.at[n, q], PARTNER, partner)
            to_across.start()
            to_partner.start()
            started += [(None, to_across), (None, to_partner)]

        if n == 0:
            loads[3].wait()
        own_sum = placed(own_pick, [sent.at[n]])
        for q in range(chunks):
            for first, rows in level_parts[q * per_chunk : (q + 1) * per_chunk]:
                part = pl.ds(first, rows)
                depth = lax.broadcasted_iota(jnp.int32, (rows, width), 0) + first
                light = jnp.exp(-0.2 * depth.astype(jnp.float32))
                c = [carried[t, part, :] for t in range(tracers)]
                bio = biology(c, [states[section, t, part, :] for t in range(tracers)], light)
                for t in range(tracers):
                    own_part = own_sum[first : first + rows, t * 128 : (t + 1) * 128]
                    adj[t, part, :] = c[t] + own_part + TIME_STEP * bio[t]
            copy_of(n, q, sent.at[n, q], ACROSS, across).wait_recv()
            on = copy_of(n, q, got.at[n, ACROSS, q], RELAYED, relay_to)
            over = copy_of(n, q, got.at[n, ACROSS, q], PASSED, partner)
            pl.when(relays)(on.start)
            pl.when(passes_across)(over.start)
            started += [(relays, on), (passes_across, over)]
        for q in range(chunks):
            copy_of(n, q, sent.at[n, q], PARTNER, partner).wait_recv()
        if n == 0:
            targets = jnp.where(
                lane < slots_pad,
                got[0, PARTNER, 0, pl.ds(body, 8), :],
                got[0, ACROSS, 0, pl.ds(body, 8), :],
            )
            near_pick = pick_of(targets[0:1, : 2 * slots_pad])
        near_sum = placed(near_pick, [got.at[n, PARTNER], got.at[n, ACROSS]])
        for t in range(tracers):
            adj[t] = adj[t] + near_sum[:, t * 128 : (t + 1) * 128]
        for q in range(chunks):
            come = copy_of(n, q, got.at[n, ACROSS, q], RELAYED, relay_to)
            pl.when(relayed)(come.wait_recv)
            over = copy_of(n, q, got.at[n, RELAYED, q], PASSED, partner)
            pl.when(passes_relayed)(over.start)
            started.append((passes_relayed, over))
        for q in range(chunks):
            come = copy_of(n, q, got.at[n, ACROSS, q], PASSED, partner)
            pl.when(gets_passed)(come.wait_recv)
        if n == 0:
            targets = jnp.where(
                lane < slots_pad,
                got[0, RELAYED, 0, pl.ds(body, 8), :],
                got[0, PASSED, 0, pl.ds(body, 8), :],
            )
            far_pick = pick_of(targets[0:1, : 2 * slots_pad])
        far_sum = placed(far_pick, [got.at[n, RELAYED], got.at[n, PASSED]])
        mask = wet(0, levels)
        for t in range(tracers):
            value = mask * (adj[t] + far_sum[:, t * 128 : (t + 1) * 128])
            if n == STEPS - 1:
                out_ref[t] = value
            else:
                adj[t] = value
    for condition, copy in started:
        if condition is None:
            copy.wait_send()
        else:
            pl.when(condition)(copy.wait_send)


def shards(peers, final_adjoint, states, implicit, wet_levels, tile_rows, tile_cols, tiles, tile_count):
    tracers, levels, width = final_adjoint.shape
    blocks = levels * width // 128
    slots = tiles.shape[0]
    chunks = -(-slots // CHUNK)
    rows = (tracers + 1) * CHUNK
    hbm = pl.BlockSpec(memory_space=pl.ANY)
    smem = pl.BlockSpec(memory_space=pltpu.SMEM)
    vmem = pl.BlockSpec(memory_space=pltpu.VMEM)
    f32 = jnp.float32
    return pl.pallas_call(
        functools.partial(kernel, peers, slots, chunks, blocks),
        out_shape=jax.ShapeDtypeStruct((tracers, levels, width), f32),
        in_specs=[hbm, hbm, hbm, vmem, smem, smem, hbm, smem],
        out_specs=vmem,
        scratch_shapes=[
            pltpu.VMEM((tracers, levels, width), f32),
            pltpu.VMEM(states.shape, f32),
            pltpu.VMEM(implicit.shape, f32),
            pltpu.VMEM(tiles.shape, tiles.dtype),
            pltpu.VMEM((tracers, levels, width), f32),
            pltpu.VMEM((blocks, 8, 128), f32),
            pltpu.VMEM((STEPS, chunks, rows, 128), f32),
            pltpu.VMEM((STEPS, 4, chunks, rows, 128), f32),
            pltpu.SemaphoreType.DMA((4,)),
            pltpu.SemaphoreType.DMA((STEPS, 4, chunks)),
            pltpu.SemaphoreType.DMA((STEPS, 4, chunks)),
        ],
        compiler_params=pltpu.CompilerParams(
            collective_id=0, has_side_effects=True, vmem_limit_bytes=60 * 1024 * 1024
        ),
    )(
        final_adjoint, states, implicit, wet_levels.reshape(1, width),
        tile_rows, tile_cols, tiles, tile_count,
    )


def solution(mesh):
    in_specs = (
        P(None, None, "col"),
        P(None, None, None, "col"),
        P(None, None, "col"),
        P("col"),
        P("col"),
        P("col"),
        P("col", None, None),
        P("col"),
    )
    out_specs = P(None, None, "col")
    return jax.shard_map(
        functools.partial(shards, mesh.shape["col"]),
        mesh=mesh, in_specs=in_specs, out_specs=out_specs, check_vma=False,
    )
```

time: 42.7 us -> 34.2 us (0.80)
  the two profiles are of different devices: /device:TPU:1 before, /device:TPU:7 now
where the time goes in v2:
time: 34.2 us; the launch traced here: 34 us
  Pallas kernels  31.7 us (93%)
  local copies, waits for them, and re-layouts  1.62 us (5%)
  between operations  0.66 us (2%)
    pallas_call x1, Pallas kernels, shards(): pl.pallas_call(functools.partial(kernel, peers, slots, chunks, blocks), o...  31.7 us
    unnamed x1, local copies, waits for them, and re-layouts  1.62 us

profile of v2, /device:TPU:7, one launch (start us, length us, event | category | flops | bytes accessed | tf_op | source)
XLA Modules:
  0.0 34.0 jit_solution(523512089705179442)
XLA Ops:
  0.7 31.7 %shard_map.82 = f32[7,50,128]{2,1,0:T(8,128)} custom-call(f32[7,50,128]{2,1,0:T(8,128)} %adj_hbm.1, f32[3,7,50,128]{3,2,1,0:T(8,128)} %states_hbm.1, f32[50,50,128]{2,1,0:T(8,128)} %imp_hbm.1, s32[1,128]{1,0:T(1,128)} %bitcast.1, s32[30]{0:T(128)} %rows_ref.1, s32[30]{0:T(128)} %cols_ref.1, bf16[30,128,128]{2,1,0:T(8,128)(2,1)} %tiles_hbm.1, ...), custom_call_target="tpu_custom_call" | custom-call | tf_op jit(solution)/shard_map/pallas_call | solution.py:267
  32.4 1.6 %copy.11 = f32[7,50,128]{2,1,0:T(8,128)} copy(f32[7,50,128]{2,1,0:T(8,128)} %shard_map.82) | data formatting | bytes 358400

commit v3 on v2

v3 whole, which is shorter than its diff:
```python
import functools

import jax
import jax.numpy as jnp
from jax import lax
from jax.experimental import pallas as pl
from jax.experimental.pallas import tpu as pltpu
from jax.sharding import PartitionSpec as P

STEPS = 3
REACH = 2
CHUNK = 16
TARGET_ROWS = 8
PARTNER, ACROSS, RELAYED, PASSED = range(4)
TIME_STEP = 0.5


def biology(c, s, light):
    phosphate, _, oxygen, plankton, grazers, detritus, nitrate = s
    inv_p = 1.0 / (0.03 + phosphate)
    inv_n = 1.0 / (0.5 + nitrate)
    inv_o = 1.0 / (1.0 + oxygen)
    square = plankton * plankton
    inv_z = 1.0 / (0.1 + square)
    up = phosphate * inv_p
    un = nitrate * inv_n
    c_growth = -c[0] + 0.1 * c[1] + 1.2 * c[2] + c[3] - 1.6 * c[6]
    c_grazing = 0.3 * c[0] - c[3] + 0.7 * c[4]
    c_mortality = 0.1 * c[1] - c[3] + 0.9 * c[5]
    c_remineral = c[0] - 1.2 * c[2] - c[5] + 1.6 * c[6]
    c_decay = c[0] - c[1] - 1.2 * c[2] + 1.6 * c[6]
    c_loss = c[5] - c[4]
    g = c_growth * (1.2 * light)
    gz = g * plankton
    q = 0.05 * c_remineral
    return (
        gz * un * (0.03 * inv_p * inv_p),
        0.17 * c_decay,
        q * detritus * (inv_o * inv_o),
        g * up * un
        + c_grazing * grazers * plankton * (0.38 * inv_z * inv_z)
        + 0.06 * c_mortality * plankton,
        1.9 * c_grazing * square * inv_z + 0.1 * c_loss * grazers,
        q * oxygen * inv_o,
        gz * up * (0.5 * inv_n * inv_n),
    )


def split(x):
    hi = x.astype(jnp.bfloat16)
    lo = (x - hi.astype(jnp.float32)).astype(jnp.bfloat16)
    return hi, lo


def tracer_groups(tracers):
    half = (tracers + 1) // 2
    return [(0, half), (half, tracers)]


def kernel(
    peers, slots, chunks, blocks,
    adj_hbm, states_hbm, imp_hbm, wet_ref, rows_ref, cols_ref, tiles_hbm, count_ref,
    early_ref, late_ref,
    adj, states, imp, tiles, carried, by_block, sent, got,
    load_sem, send_sem, recv_sem, pass_sem,
):
    tracers, levels, width = adj.shape
    groups = tracer_groups(tracers)
    half = groups[0][1]
    slots_pad = chunks * CHUNK
    body = half * CHUNK
    by_row = by_block.reshape(2, blocks * 8, 128)
    me = lax.axis_index("col")
    chip = me // 2
    core = me % 2
    odd = chip % 2
    partner = me + 1 - 2 * core
    across = me + 2 - 4 * odd
    relay_to = me + 4 - 8 * odd
    relay_from = me - 4 + 8 * odd
    beside = me - 1 + 2 * odd
    relays = (relay_to >= 0) & (relay_to < peers)
    relayed = (relay_from >= 0) & (relay_from < peers)
    passes = core == odd
    direct = passes & relayed
    gets_fourth = jnp.logical_not(passes) | relayed
    misses_fourth = passes & jnp.logical_not(relayed)

    loads = [
        pltpu.make_async_copy(src, dst, load_sem.at[i])
        for i, (src, dst) in enumerate(
            ((adj_hbm, adj), (imp_hbm, imp), (tiles_hbm, tiles), (states_hbm, states))
        )
    ]
    for load in loads:
        load.start()

    barrier = pltpu.get_barrier_semaphore()

    def greet(device):
        pl.semaphore_signal(
            barrier, inc=1, device_id=(device,), device_id_type=pl.DeviceIdType.MESH
        )

    greet(partner)
    greet(across)
    pl.when(relays)(lambda: greet(relay_to))
    pl.when(relayed)(lambda: greet(relay_from))
    pl.when(direct)(lambda: greet(beside))

    lane = lax.broadcasted_iota(jnp.int32, (TARGET_ROWS, 128), 1)
    lane_slot = lane % slots_pad
    own_ids = jnp.full((TARGET_ROWS, 128), -1, jnp.int32)
    for s in range(slots):
        own_ids = jnp.where(lane_slot == s, cols_ref[s], own_ids)
    own_ids = jnp.where(lane_slot < count_ref[0], own_ids, -1).astype(jnp.float32)
    for n in range(STEPS):
        for g in range(2):
            for s in range(slots, slots_pad):
                sent[n, g, s // CHUNK, pl.ds(s % CHUNK, half, stride=CHUNK), :] = jnp.zeros(
                    (half, 128), jnp.float32
                )
    for g in range(2):
        count = groups[g][1] - groups[g][0]
        for r in list(range(count, half)) + list(range(half + count, 8)):
            for first in range(0, blocks, 8):
                some = min(8, blocks - first)
                by_row[g, pl.ds(first * 8 + r, some, stride=8), :] = jnp.zeros(
                    (some, 128), jnp.float32
                )

    def blank(place):
        for n in range(STEPS):
            for g in range(2):
                for q in range(chunks):
                    got[n, place, g, q] = jnp.zeros(got.shape[4:], jnp.float32)
        got[0, place, 0, 0, pl.ds(body, TARGET_ROWS), :] = jnp.full(
            (TARGET_ROWS, 128), -1.0, jnp.float32
        )

    pl.when(jnp.logical_not(relayed))(lambda: blank(RELAYED))
    pl.when(misses_fourth)(lambda: blank(PASSED))

    pl.semaphore_wait(
        barrier,
        2 + relays.astype(jnp.int32) + relayed.astype(jnp.int32) + direct.astype(jnp.int32),
    )

    def copy_of(n, g, q, source, place, device, sem=None):
        size = (groups[g][1] - groups[g][0]) * CHUNK
        if n == 0 and g == 0 and q == 0:
            size = body + TARGET_ROWS
        return pltpu.make_async_remote_copy(
            src_ref=source.at[g, q, pl.ds(0, size)],
            dst_ref=got.at[n, place, g, q, pl.ds(0, size)],
            send_sem=send_sem.at[n, place, g, q] if sem is None else sem,
            recv_sem=recv_sem.at[n, place, g, q],
            device_id=(device,), device_id_type=pl.DeviceIdType.MESH,
        )

    def wet(first, rows):
        level = lax.broadcasted_iota(jnp.int32, (rows, width), 0) + first
        return (level < wet_ref[...]).astype(jnp.float32)

    def pick_of(targets):
        block = lax.broadcasted_iota(jnp.int32, (blocks, targets.shape[1]), 0) + me * blocks
        pick = (block.astype(jnp.float32) == targets).astype(jnp.bfloat16)
        return jnp.concatenate([pick, pick], axis=1)

    def placed(pick, g, sources):
        columns = []
        for t in range(groups[g][1] - groups[g][0]):
            pieces = [
                ref[g, q, pl.ds(t * CHUNK, CHUNK), :] for ref in sources for q in range(chunks)
            ]
            columns.append(jnp.concatenate(split(jnp.concatenate(pieces, axis=0)), axis=0))
        return jnp.dot(pick, jnp.concatenate(columns, axis=1), preferred_element_type=jnp.float32)

    started = []
    picks = {}

    def compute(n, g):
        begin, end = groups[g]
        acc = [None] * (end - begin)
        for k in range(levels):
            m = imp[k]
            for t in range(begin, end):
                term = m * adj[t, pl.ds(k, 1), :]
                acc[t - begin] = term if k == 0 else acc[t - begin] + term
        mask = wet(0, levels)
        for t in range(begin, end):
            value = acc[t - begin] * mask
            carried[t] = value
            hi, lo = split(value)
            for piece, row in ((hi, t - begin), (lo, t - begin + half)):
                piece = piece.astype(jnp.float32)
                for r in range(0, levels, 8):
                    some = min(8, levels - r)
                    by_row[g, pl.ds(r * 8 + row, some, stride=8), :] = piece[r : r + some]
        if n == 0 and g == 0:
            loads[2].wait()
        for q in range(chunks):
            for s in range(q * CHUNK, min(slots, (q + 1) * CHUNK)):
                row = jnp.minimum(jnp.maximum(rows_ref[s] - me * blocks, 0), blocks - 1)
                both = jnp.dot(
                    by_block[g, row].astype(jnp.bfloat16), tiles[s],
                    preferred_element_type=jnp.float32,
                )
                sent[n, g, q, pl.ds(s % CHUNK, half, stride=CHUNK), :] = (
                    both[:half] + both[half : 2 * half]
                )
            if n == 0 and g == 0 and q == 0:
                sent[0, 0, 0, pl.ds(body, TARGET_ROWS), :] = own_ids
            copy = copy_of(n, g, q, sent.at[n], ACROSS, across)
            copy.start()
            started.append((None, copy))
        for q in range(chunks):
            near = copy_of(n, g, q, sent.at[n], PARTNER, partner)
            near.start()
            far = copy_of(n, g, q, sent.at[n], PASSED, beside)
            pl.when(direct)(far.start)
            started.extend([(None, near), (direct, far)])

    def grow(n):
        section = STEPS - 1 - n
        if n == 0:
            loads[3].wait()
        for first in range(0, levels, 8):
            rows = min(8, levels - first)
            part = pl.ds(first, rows)
            depth = lax.broadcasted_iota(jnp.int32, (rows, width), 0) + first
            light = jnp.exp(-0.2 * depth.astype(jnp.float32))
            c = [carried[t, part, :] for t in range(tracers)]
            bio = biology(c, [states[section, t, part, :] for t in range(tracers)], light)
            for t in range(tracers):
                adj[t, part, :] = c[t] + TIME_STEP * bio[t]

    def forward(n, g):
        for q in range(chunks):
            copy_of(n, g, q, sent.at[n], ACROSS, across).wait_recv()
            on = copy_of(n, g, q, got.at[n, ACROSS], RELAYED, relay_to)
            over = copy_of(n, g, q, got.at[n, ACROSS], PASSED, partner, pass_sem.at[n, g, q])
            pl.when(relays)(on.start)
            pl.when(passes)(over.start)
            started.extend([(relays, on), (passes, over)])

    def two(n, first, second):
        return jnp.where(
            lane < slots_pad,
            first[0, 0, pl.ds(body, TARGET_ROWS), :],
            second[0, 0, pl.ds(body, TARGET_ROWS), :],
        )

    def near(n, g):
        for q in range(chunks):
            copy_of(n, g, q, sent.at[n], PARTNER, partner).wait_recv()
        if "near" not in picks:
            ids = two(n, sent.at[0], got.at[0, PARTNER])
            ids = jnp.where(
                lane < 2 * slots_pad, ids, got[0, ACROSS, 0, 0, pl.ds(body, TARGET_ROWS), :]
            )
            picks["near"] = pick_of(ids[0:1, : 3 * slots_pad])
        total = placed(
            picks["near"], g, [sent.at[n], got.at[n, PARTNER], got.at[n, ACROSS]]
        )
        for i, t in enumerate(range(*groups[g])):
            adj[t] = adj[t] + total[:, i * 128 : (i + 1) * 128]

    def finish(n, g):
        for q in range(chunks):
            come = copy_of(n, g, q, got.at[n, ACROSS], RELAYED, relay_to)
            pl.when(relayed)(come.wait_recv)
            fourth = copy_of(n, g, q, sent.at[n], PASSED, beside)
            pl.when(gets_fourth)(fourth.wait_recv)
        if "far" not in picks:
            ids = two(n, got.at[0, RELAYED], got.at[0, PASSED])
            picks["far"] = pick_of(ids[0:1, : 2 * slots_pad])
        total = placed(picks["far"], g, [got.at[n, RELAYED], got.at[n, PASSED]])
        mask = wet(0, levels)
        for i, t in enumerate(range(*groups[g])):
            late = total[:, i * 128 : (i + 1) * 128]
            if n == STEPS - 1:
                early_ref[t] = mask * adj[t]
                late_ref[t] = mask * late
            else:
                adj[t] = mask * (adj[t] + late)

    loads[0].wait()
    loads[1].wait()
    compute(0, 0)
    compute(0, 1)
    grow(0)
    for n in range(STEPS):
        forward(n, 0)
        near(n, 0)
        forward(n, 1)
        near(n, 1)
        finish(n, 0)
        if n < STEPS - 1:
            compute(n + 1, 0)
        finish(n, 1)
        if n < STEPS - 1:
            compute(n + 1, 1)
            grow(n + 1)
    for condition, copy in started:
        if condition is None:
            copy.wait_send()
        else:
            pl.when(condition)(copy.wait_send)


def shards(peers, final_adjoint, states, implicit, wet_levels, tile_rows, tile_cols, tiles, tile_count):
    tracers, levels, width = final_adjoint.shape
    blocks = levels * width // 128
    slots = tiles.shape[0]
    chunks = -(-slots // CHUNK)
    rows = tracer_groups(tracers)[0][1] * CHUNK + TARGET_ROWS
    hbm = pl.BlockSpec(memory_space=pl.ANY)
    smem = pl.BlockSpec(memory_space=pltpu.SMEM)
    vmem = pl.BlockSpec(memory_space=pltpu.VMEM)
    f32 = jnp.float32
    early, late = pl.pallas_call(
        functools.partial(kernel, peers, slots, chunks, blocks),
        out_shape=[jax.ShapeDtypeStruct((tracers, levels, width), f32)] * 2,
        in_specs=[hbm, hbm, hbm, vmem, smem, smem, hbm, smem],
        out_specs=[vmem, vmem],
        scratch_shapes=[
            pltpu.VMEM((tracers, levels, width), f32),
            pltpu.VMEM(states.shape, f32),
            pltpu.VMEM(implicit.shape, f32),
            pltpu.VMEM(tiles.shape, tiles.dtype),
            pltpu.VMEM((tracers, levels, width), f32),
            pltpu.VMEM((2, blocks, 8, 128), f32),
            pltpu.VMEM((STEPS, 2, chunks, rows, 128), f32),
            pltpu.VMEM((STEPS, 4, 2, chunks, rows, 128), f32),
            pltpu.SemaphoreType.DMA((4,)),
            pltpu.SemaphoreType.DMA((STEPS, 4, 2, chunks)),
            pltpu.SemaphoreType.DMA((STEPS, 4, 2, chunks)),
            pltpu.SemaphoreType.DMA((STEPS, 2, chunks)),
        ],
        compiler_params=pltpu.CompilerParams(
            collective_id=0, has_side_effects=True, vmem_limit_bytes=60 * 1024 * 1024
        ),
    )(
        final_adjoint, states, implicit, wet_levels.reshape(1, width),
        tile_rows, tile_cols, tiles, tile_count,
    )
    return early + late


def solution(mesh):
    in_specs = (
        P(None, None, "col"),
        P(None, None, None, "col"),
        P(None, None, "col"),
        P("col"),
        P("col"),
        P("col"),
        P("col", None, None),
        P("col"),
    )
    out_specs = P(None, None, "col")
    return jax.shard_map(
        functools.partial(shards, mesh.shape["col"]),
        mesh=mesh, in_specs=in_specs, out_specs=out_specs, check_vma=False,
    )
```

time: 34.2 us -> 32.6 us (0.953)
  the two profiles are of different devices: /device:TPU:7 before, /device:TPU:16 now
where the time goes in v3:
time: 32.6 us; the launch traced here: 32.4 us
  Pallas kernels  30 us (92%)
  other arithmetic  1.73 us (5%)
  between operations  0.66 us (2%)
    pallas_call x1, Pallas kernels, shards(): pl.pallas_call(functools.partial(kernel, peers, slots, chunks, blocks), o...  30 us
    add x1, other arithmetic, shards(): return early + late  1.73 us

profile of v3, /device:TPU:16, one launch (start us, length us, event | category | flops | bytes accessed | tf_op | source)
XLA Modules:
  0.0 32.4 jit_solution(10825787588973789555)
XLA Ops:
  0.7 30.0 %shard_map.82 = (f32[7,50,128]{2,1,0:T(8,128)}, f32[7,50,128]{2,1,0:T(8,128)}) custom-call(f32[7,50,128]{2,1,0:T(8,128)} %adj_hbm.1, f32[3,7,50,128]{3,2,1,0:T(8,128)} %states_hbm.1, f32[50,50,128]{2,1,0:T(8,128)} %imp_hbm.1, s32[1,128]{1,0:T(1,128)} %bitcast.1, s32[30]{0:T(128)} %rows_ref.1, s32[30]{0:T(128)} %cols_ref.1, bf16[30,128,128]{2,1,0:T(8,128)(2,1)} %tiles_hbm.1, ...), custom_call_target="tpu_custom_call" | custom-call | tf_op jit(solution)/shard_map/pallas_call | solution.py:322
  30.7 1.7 %add.3 = f32[7,50,128]{2,1,0:T(8,128)} add(f32[7,50,128]{2,1,0:T(8,128)} %get-tuple-element.7, f32[7,50,128]{2,1,0:T(8,128)} %get-tuple-element.8) | non-fusion elementwise | flops 44800 | bytes 537600 | tf_op jit(solution)/shard_map/add | solution.py:348

commit v4 on v3

--- a/solution.py
+++ b/solution.py
@@ -200,15 +200,29 @@
         if n == 0 and g == 0:
             loads[2].wait()
         for q in range(chunks):
-            for s in range(q * CHUNK, min(slots, (q + 1) * CHUNK)):
-                row = jnp.minimum(jnp.maximum(rows_ref[s] - me * blocks, 0), blocks - 1)
-                both = jnp.dot(
-                    by_block[g, row].astype(jnp.bfloat16), tiles[s],
+            last = min(slots, (q + 1) * CHUNK)
+            for s in range(q * CHUNK, last, 4):
+                some = list(range(s, min(s + 4, last)))
+                zero = jnp.zeros((8, 128), jnp.bfloat16)
+                lines, sides = [], []
+                for i, slot in enumerate(some):
+                    row = jnp.minimum(jnp.maximum(rows_ref[slot] - me * blocks, 0), blocks - 1)
+                    x = by_block[g, row].astype(jnp.bfloat16)
+                    lines.append(jnp.concatenate([zero, x] if i % 2 else [x, zero], axis=1))
+                for i in range(0, len(some), 2):
+                    pair = [tiles[slot] for slot in some[i : i + 2]]
+                    if len(pair) == 1:
+                        pair.append(jnp.zeros_like(pair[0]))
+                    sides.append(jnp.concatenate(pair, axis=0))
+                product = jnp.dot(
+                    jnp.concatenate(lines, axis=0), jnp.concatenate(sides, axis=1),
                     preferred_element_type=jnp.float32,
                 )
-                sent[n, g, q, pl.ds(s % CHUNK, half, stride=CHUNK), :] = (
-                    both[:half] + both[half : 2 * half]
-                )
+                for i, slot in enumerate(some):
+                    both = product[8 * i : 8 * i + 8, i // 2 * 128 : i // 2 * 128 + 128]
+                    sent[n, g, q, pl.ds(slot % CHUNK, half, stride=CHUNK), :] = (
+                        both[:half] + both[half : 2 * half]
+                    )
             if n == 0 and g == 0 and q == 0:
                 sent[0, 0, 0, pl.ds(body, TARGET_ROWS), :] = own_ids
             copy = copy_of(n, g, q, sent.at[n], ACROSS, across)

time: 32.6 us -> 32.4 us (level)
  no operation moved by 1% of the time
where the time goes in v4:
time: 32.4 us; the launch traced here: 32.2 us
  Pallas kernels  29.8 us (92%)
  other arithmetic  1.73 us (5%)
  between operations  0.66 us (2%)
    pallas_call x1, Pallas kernels, shards(): pl.pallas_call(functools.partial(kernel, peers, slots, chunks, blocks), o...  29.8 us
    add x1, other arithmetic, shards(): return early + late  1.73 us

profile of v4, /device:TPU:16, one launch (start us, length us, event | category | flops | bytes accessed | tf_op | source)
XLA Modules:
  0.0 32.2 jit_solution(5617912120218697939)
XLA Ops:
  0.7 29.8 %shard_map.82 = (f32[7,50,128]{2,1,0:T(8,128)}, f32[7,50,128]{2,1,0:T(8,128)}) custom-call(f32[7,50,128]{2,1,0:T(8,128)} %adj_hbm.1, f32[3,7,50,128]{3,2,1,0:T(8,128)} %states_hbm.1, f32[50,50,128]{2,1,0:T(8,128)} %imp_hbm.1, s32[1,128]{1,0:T(1,128)} %bitcast.1, s32[30]{0:T(128)} %rows_ref.1, s32[30]{0:T(128)} %cols_ref.1, bf16[30,128,128]{2,1,0:T(8,128)(2,1)} %tiles_hbm.1, ...), custom_call_target="tpu_custom_call" | custom-call | tf_op jit(solution)/shard_map/pallas_call | solution.py:336
  30.5 1.7 %add.3 = f32[7,50,128]{2,1,0:T(8,128)} add(f32[7,50,128]{2,1,0:T(8,128)} %get-tuple-element.7, f32[7,50,128]{2,1,0:T(8,128)} %get-tuple-element.8) | non-fusion elementwise | flops 44800 | bytes 537600 | tf_op jit(solution)/shard_map/add | solution.py:362

commit v5 on v4

--- a/solution.py
+++ b/solution.py
@@ -60,7 +60,7 @@
 def kernel(
     peers, slots, chunks, blocks,
     adj_hbm, states_hbm, imp_hbm, wet_ref, rows_ref, cols_ref, tiles_hbm, count_ref,
-    early_ref, late_ref,
+    out_ref,
     adj, states, imp, tiles, carried, by_block, sent, got,
     load_sem, send_sem, recv_sem, pass_sem,
 ):
@@ -78,11 +78,10 @@
     across = me + 2 - 4 * odd
     relay_to = me + 4 - 8 * odd
     relay_from = me - 4 + 8 * odd
-    beside = me - 1 + 2 * odd
     relays = (relay_to >= 0) & (relay_to < peers)
     relayed = (relay_from >= 0) & (relay_from < peers)
     passes = core == odd
-    direct = passes & relayed
+    passes_relayed = jnp.logical_not(passes) & relayed
     gets_fourth = jnp.logical_not(passes) | relayed
     misses_fourth = passes & jnp.logical_not(relayed)
 
@@ -106,7 +105,6 @@
     greet(across)
     pl.when(relays)(lambda: greet(relay_to))
     pl.when(relayed)(lambda: greet(relay_from))
-    pl.when(direct)(lambda: greet(beside))
 
     lane = lax.broadcasted_iota(jnp.int32, (TARGET_ROWS, 128), 1)
     lane_slot = lane % slots_pad
@@ -143,7 +141,7 @@
 
     pl.semaphore_wait(
         barrier,
-        2 + relays.astype(jnp.int32) + relayed.astype(jnp.int32) + direct.astype(jnp.int32),
+        2 + relays.astype(jnp.int32) + relayed.astype(jnp.int32),
     )
 
     def copy_of(n, g, q, source, place, device, sem=None):
@@ -231,9 +229,7 @@
         for q in range(chunks):
             near = copy_of(n, g, q, sent.at[n], PARTNER, partner)
             near.start()
-            far = copy_of(n, g, q, sent.at[n], PASSED, beside)
-            pl.when(direct)(far.start)
-            started.extend([(None, near), (direct, far)])
+            started.append((None, near))
 
     def grow(n):
         section = STEPS - 1 - n
@@ -284,7 +280,11 @@
         for q in range(chunks):
             come = copy_of(n, g, q, got.at[n, ACROSS], RELAYED, relay_to)
             pl.when(relayed)(come.wait_recv)
-            fourth = copy_of(n, g, q, sent.at[n], PASSED, beside)
+            over = copy_of(n, g, q, got.at[n, RELAYED], PASSED, partner, pass_sem.at[n, g, q])
+            pl.when(passes_relayed)(over.start)
+            started.append((passes_relayed, over))
+        for q in range(chunks):
+            fourth = copy_of(n, g, q, got.at[n, ACROSS], PASSED, partner)
             pl.when(gets_fourth)(fourth.wait_recv)
         if "far" not in picks:
             ids = two(n, got.at[0, RELAYED], got.at[0, PASSED])
@@ -294,8 +294,7 @@
         for i, t in enumerate(range(*groups[g])):
             late = total[:, i * 128 : (i + 1) * 128]
             if n == STEPS - 1:
-                early_ref[t] = mask * adj[t]
-                late_ref[t] = mask * late
+                out_ref[t] = mask * (adj[t] + late)
             else:
                 adj[t] = mask * (adj[t] + late)
 
@@ -333,11 +332,11 @@
     smem = pl.BlockSpec(memory_space=pltpu.SMEM)
     vmem = pl.BlockSpec(memory_space=pltpu.VMEM)
     f32 = jnp.float32
-    early, late = pl.pallas_call(
+    return pl.pallas_call(
         functools.partial(kernel, peers, slots, chunks, blocks),
-        out_shape=[jax.ShapeDtypeStruct((tracers, levels, width), f32)] * 2,
+        out_shape=jax.ShapeDtypeStruct((tracers, levels, width), f32),
         in_specs=[hbm, hbm, hbm, vmem, smem, smem, hbm, smem],
-        out_specs=[vmem, vmem],
+        out_specs=vmem,
         scratch_shapes=[
             pltpu.VMEM((tracers, levels, width), f32),
             pltpu.VMEM(states.shape, f32),
@@ -359,7 +358,6 @@
         final_adjoint, states, implicit, wet_levels.reshape(1, width),
         tile_rows, tile_cols, tiles, tile_count,
     )
-    return early + late
 
 
 def solution(mesh):

time: 32.4 us -> 32.5 us (level)
  the two profiles are of different devices: /device:TPU:16 before, /device:TPU:7 now
where the time goes in v5:
time: 32.5 us; the launch traced here: 32.3 us
  Pallas kernels  30.1 us (93%)
  local copies, waits for them, and re-layouts  1.62 us (5%)
  between operations  0.66 us (2%)
    pallas_call x1, Pallas kernels, shards(): pl.pallas_call(functools.partial(kernel, peers, slots, chunks, blocks), o...  30.1 us
    unnamed x1, local copies, waits for them, and re-layouts  1.62 us

profile of v5, /device:TPU:7, one launch (start us, length us, event | category | flops | bytes accessed | tf_op | source)
XLA Modules:
  0.0 32.3 jit_solution(10715246289217281157)
XLA Ops:
  0.7 30.1 %shard_map.82 = f32[7,50,128]{2,1,0:T(8,128)} custom-call(f32[7,50,128]{2,1,0:T(8,128)} %adj_hbm.1, f32[3,7,50,128]{3,2,1,0:T(8,128)} %states_hbm.1, f32[50,50,128]{2,1,0:T(8,128)} %imp_hbm.1, s32[1,128]{1,0:T(1,128)} %bitcast.1, s32[30]{0:T(128)} %rows_ref.1, s32[30]{0:T(128)} %cols_ref.1, bf16[30,128,128]{2,1,0:T(8,128)(2,1)} %tiles_hbm.1, ...), custom_call_target="tpu_custom_call" | custom-call | tf_op jit(solution)/shard_map/pallas_call | solution.py:335
  30.7 1.6 %copy.11 = f32[7,50,128]{2,1,0:T(8,128)} copy(f32[7,50,128]{2,1,0:T(8,128)} %shard_map.82) | data formatting | bytes 358400
